TPU v7x, 256 devices: a whole 4x4x8 slice. The times are simulated.
256 devices in a mesh: row: 16 (over z_hi, y, core), col: 16 (over z_lo, x).
Axes of the slice: x: 4, y: 4, z: 8 (z_hi: 2, z_lo: 4; z = z_hi * 4 + z_lo), core: 2. Of those that a mesh axis runs over, the one named last changes fastest.
Arguments:
- inputs: bfloat16 [512, 9216], P('col', 'row'), may hold values from -6 to 6
- out_grad: bfloat16 [512, 9216], P('col', 'row'), may hold values from -6 to 6
- w_up: bfloat16 [9216, 36864], P('row', 'col'), may hold values from -0.0625 to 0.0625
- w_down: bfloat16 [36864, 9216], P('col', 'row'), may hold values from -0.0625 to 0.0625
Outputs:
- input_grad: bfloat16 [512, 9216], P('col', 'row')
- up_grad: bfloat16 [9216, 36864], P('row', 'col')
- down_grad: bfloat16 [36864, 9216], P('col', 'row')
All inputs are finite; a program needn't handle non-finite values.
Results may differ from a plain program's by a relative error of at most 0.0049.
Values may be sent and summed in bfloat16 or wider, within the bound.
A program may use at most 128 MiB of HBM per device.

v0:
```python
import jax
import jax.numpy as jnp
from jax import lax
from jax.sharding import PartitionSpec as P


def activate(preact, hidden_grad):
    positive = jnp.maximum(preact, 0.0)
    hidden = (positive * positive).astype(jnp.bfloat16)
    preact_grad = (hidden_grad * 2.0 * positive).astype(jnp.bfloat16)
    return (hidden, preact_grad)


def shards(inputs, out_grad, w_up, w_down):
    input_rows, grad_rows = (
        lax.all_gather(inputs, "col", axis=0, tiled=True),
        lax.all_gather(out_grad, "col", axis=0, tiled=True),
    )
    up_part = jnp.dot(input_rows, w_up, preferred_element_type=jnp.float32)
    back_part = lax.dot_general(
        grad_rows, w_down, (((1,), (1,)), ((), ())), preferred_element_type=jnp.float32
    )
    preact, hidden_grad = (
        lax.psum_scatter(up_part, "row", scatter_dimension=0, tiled=True),
        lax.psum_scatter(back_part, "row", scatter_dimension=0, tiled=True),
    )
    hidden_share, grad_share = activate(preact, hidden_grad)
    hidden, preact_grad = (
        lax.all_gather(hidden_share, "row", axis=0, tiled=True),
        lax.all_gather(grad_share, "row", axis=0, tiled=True),
    )
    down_grad = lax.dot_general(
        hidden, grad_rows, (((0,), (0,)), ((), ())), preferred_element_type=jnp.float32
    )
    up_grad = lax.dot_general(
        input_rows, preact_grad, (((0,), (0,)), ((), ())), preferred_element_type=jnp.float32
    )
    input_grad = lax.psum_scatter(
        lax.dot_general(
            preact_grad, w_up, (((1,), (1,)), ((), ())), preferred_element_type=jnp.float32
        ),
        "col",
        scatter_dimension=0,
        tiled=True,
    )
    return (
        input_grad.astype(jnp.bfloat16),
        up_grad.astype(jnp.bfloat16),
        down_grad.astype(jnp.bfloat16),
    )


def solution(mesh):
    in_specs = (P("col", "row"), P("col", "row"), P("row", "col"), P("col", "row"))
    out_specs = (P("col", "row"), P("row", "col"), P("col", "row"))
    return jax.shard_map(shards, mesh=mesh, in_specs=in_specs, out_specs=out_specs, check_vma=False)
```

profile of v0, /device:TPU:16, one launch (start us, length us, event | category | flops | bytes accessed | tf_op | source)
XLA Modules:
  0.0 494.5 jit_solution(12837284402303959361)
XLA Ops:
  7.2 0.0 reduce-scatter.6.cloned.1.call-start
  7.2 47.7 %all_gather.13 = bf16[512,576]{1,0:T(8,128)(2,1)S(1)} all-gather(bf16[32,576]{1,0:T(8,128)(2,1)} %param.4), channel_id=1, replica_groups=mesh['row'=16,'col'=16] {'col'}, dimensions={0}, use_global_device_ids=true | all-gather | bytes 626688 | tf_op jit(solution)/shard_map/all_gather | solution.py:16
  54.9 4.1 fusion.2
  59.1 0.0 reduce-scatter.6.cloned.1.call-update
  59.1 0.0 reduce-scatter.4.cloned.1.call-start
  59.2 0.7 copy-done.2
  59.9 40.4 %all_gather.12 = bf16[512,576]{1,0:T(8,128)(2,1)S(1)} all-gather(bf16[32,576]{1,0:T(8,128)(2,1)S(1)} %copy-done.2), channel_id=1, replica_groups=mesh['row'=16,'col'=16] {'col'}, dimensions={0}, use_global_device_ids=true | all-gather | bytes 626688 | tf_op jit(solution)/shard_map/all_gather | solution.py:17
  100.3 0.8 copy-done.1
  101.1 5.9 %fusion.1 = f32[512,2304]{1,0:T(8,128)} fusion(bf16[512,576]{1,0:T(8,128)(2,1)S(1)} %all_gather.12, bf16[2304,576]{0,1:T(8,128)(2,1)} %param.7), kind=kOutput, calls=%fused_computation.5 | convolution fusion | flops 1358954496 | bytes 7962624 | tf_op jit(solution)/shard_map/dot_general | solution.py:20
  107.1 0.0 all-gather.3.cloned.1.call-start
  107.2 56.7 %reduce-scatter.6.cloned.1.call-done = f32[32,2304]{1,0:T(8,128)} async-done(((f32[512,2304]{1,0:T(8,128)}), f32[32,2304]{1,0:T(8,128)}) %reduce-scatter.6.cloned.1.call-update) | async-done | bytes 294928 | tf_op jit(solution)/shard_map/reduce_scatter | solution.py:24
  163.8 109.1 %reduce-scatter.4.cloned.1.call-done = f32[32,2304]{1,0:T(8,128)} async-done(((f32[512,2304]{1,0:T(8,128)}), f32[32,2304]{1,0:T(8,128)}) %reduce-scatter.4.cloned.1.call-update) | async-done | bytes 294928 | tf_op jit(solution)/shard_map/reduce_scatter | solution.py:25
  272.9 1.8 multiply_convert_fusion
  274.7 0.0 all-gather.3.cloned.1.call-update
  274.7 0.0 all-gather.5.cloned.1.call-start
  274.8 0.5 all-gather.5.cloned.1.call-update
  275.3 0.0 reduce-scatter.8.cloned.1.call-start
  275.4 61.4 %all-gather.3.cloned.1.call-done = bf16[512,2304]{1,0:T(8,128)(2,1)} async-done(((bf16[32,2304]{1,0:T(8,128)(2,1)}), bf16[512,2304]{1,0:T(8,128)(2,1)}) %all-gather.3.cloned.1.call-update) | async-done | bytes 2359312 | tf_op jit(solution)/shard_map/all_gather | solution.py:30
  336.7 4.8 fusion.3
  341.5 4.8 fusion
  346.3 54.3 %all-gather.5.cloned.1.call-done = bf16[512,2304]{1,0:T(8,128)(2,1)} async-done(((bf16[32,2304]{1,0:T(8,128)(2,1)}), bf16[512,2304]{1,0:T(8,128)(2,1)}) %all-gather.5.cloned.1.call-update) | async-done | bytes 2359312 | tf_op jit(solution)/shard_map/all_gather | solution.py:29
  400.5 4.9 convolution_convert_fusion
  405.4 81.0 %reduce-scatter.8.cloned.1.call-done = f32[32,576]{1,0:T(8,128)} async-done(((f32[512,576]{1,0:T(8,128)}), f32[32,576]{1,0:T(8,128)}) %reduce-scatter.8.cloned.1.call-update) | async-done | bytes 73744 | tf_op jit(solution)/shard_map/reduce_scatter | solution.py:38
  486.5 1.5 convert_element_type.19
  (6 shorter events, 0.0 us)
Async XLA Ops:
  7.2 47.8 %copy-start = (bf16[576,2304]{1,0:T(8,128)(2,1)S(1)}, bf16[576,2304]{1,0:T(8,128)(2,1)}, u32[]{:S(2)}) copy-start(bf16[576,2304]{1,0:T(8,128)(2,1)} %param.6) | copy-start | bytes 7962628
  7.2 156.6 %reduce-scatter.6.cloned.1.call-start = ((), (), s32[]{:S(2)}) async-start(), calls=%async_computation.4 | async-start | bytes 5013504 | tf_op jit(solution)/shard_map/reduce_scatter | solution.py:24
  59.1 0.8 copy-start.2
  59.1 213.8 %reduce-scatter.4.cloned.1.call-start = ((), (), s32[]{:S(2)}) async-start(), calls=%async_computation.3 | async-start | bytes 5013504 | tf_op jit(solution)/shard_map/reduce_scatter | solution.py:25
  100.3 0.8 copy-start.1
  107.1 229.6 %all-gather.3.cloned.1.call-start = ((), (), s32[]{:S(2)}) async-start(), calls=%async_computation.5 | async-start | bytes 2506752 | tf_op jit(solution)/shard_map/all_gather | solution.py:30
  274.7 125.8 %all-gather.5.cloned.1.call-start = ((), (), s32[]{:S(2)}) async-start(), calls=%async_computation.7 | async-start | bytes 2506752 | tf_op jit(solution)/shard_map/all_gather | solution.py:29
  275.3 211.1 %reduce-scatter.8.cloned.1.call-start = ((), (), s32[]{:S(2)}) async-start(), calls=%async_computation.6 | async-start | bytes 1392640 | tf_op jit(solution)/shard_map/reduce_scatter | solution.py:38
Sparse Core Ops, SparseCore 0:
  59.2 104.5 reduce-scatter.5
  168.8 104.0 reduce-scatter.3
  276.2 60.4 all-gather.2
  339.9 60.6 all-gather.4
  402.9 83.4 reduce-scatter.7
where the time goes:
time: 495 us; the launch traced here: 494 us
  waiting for transfers between devices  363 us (73%)
  blocking collectives  88.1 us (18%)
  matrix products  24.5 us (5%)
  between operations  13.8 us (3%)
    reduce_scatter x1, waiting for transfers between devices, shards(): lax.psum_scatter(back_part, 'row', scatter_dimension=0, tiled=True)  109 us
    reduce_scatter x1, waiting for transfers between devices, shards(): lax.psum_scatter(lax.dot_general(preact_grad, w_up, (((1,), (1,)), ((), (...  81 us
    all_gather x1, waiting for transfers between devices, shards(): lax.all_gather(grad_share, 'row', axis=0, tiled=True)  61.4 us
    reduce_scatter x1, waiting for transfers between devices, shards(): lax.psum_scatter(up_part, 'row', scatter_dimension=0, tiled=True)  56.7 us
    all_gather x1, waiting for transfers between devices, shards(): lax.all_gather(hidden_share, 'row', axis=0, tiled=True)  54.3 us
    all_gather x1, blocking collectives, shards(): lax.all_gather(inputs, 'col', axis=0, tiled=True)  47.7 us
    all_gather x1, blocking collectives, shards(): lax.all_gather(out_grad, 'col', axis=0, tiled=True)  40.4 us
  transfers between devices with their start and end apart: 5, of which 5 were waited for; matrix products, arithmetic and copies ran while one was open for 4% of the time, Pallas kernels for 0%

commit v1 on v0

v1 whole, which is shorter than its diff:
```python
import functools

import jax
import jax.numpy as jnp
from jax import lax
from jax.experimental import pallas as pl
from jax.experimental.pallas import tpu as pltpu
from jax.sharding import PartitionSpec as P

MESH = pl.DeviceIdType.MESH
F32, BF16 = jnp.float32, jnp.bfloat16

PLANES = 4
BLOCK = 32
CHUNK = 128
FEATS = 576
HALF = 1152

ORDER = (
    "U00 U01 C00 P1".split()
    + "P2 C01 P3 R00".split()
    + "U10 R01 U11 C10".split()
    + "U20 Z00 C11 U21".split()
    + "Z01 C20 R10 U30".split()
    + "C21 U31 R11 C30".split()
    + "R20 C31 A00 Z10".split()
    + "R21 Z11 T A01".split()
    + "R30 Z20 R31 A10".split()
    + "H00 F00 Z21 H01".split()
    + "A11 F01 Z30 Z31".split()
    + "A20 F10 H10 E00".split()
    + "F11 A21 H11 E01".split()
    + "I0 F20 H20 A30".split()
    + "E10 E11 I1 A31".split()
    + "H21 F21 E20 H30".split()
    + "J0 F30 F31 H31".split()
    + "J1 E21 E30 I2".split()
    + "E31 I3 G0 J2".split()
    + "J3 G1".split()
)

NAMES = (
    [f"gz{k}" for k in (1, 2, 3)]
    + [f"gx{k}{m}{d}" for k in range(4) for m in range(2) for d in range(3)]
    + [f"{s}{k}{m}" for s in "c r p q z au ad".split() for k in range(4) for m in range(2)]
    + [f"{s}{k}{m}" for s in "ac f fc hc ec".split() for k in range(4) for m in range(2)]
    + [f"ix{k}{d}" for k in range(4) for d in range(3)]
    + [f"iz{k}" for k in (1, 2, 3)]
)
SLOT = {name: i for i, name in enumerate(NAMES)}


def nt(a, b):
    return lax.dot_general(a, b, (((1,), (1,)), ((), ())), preferred_element_type=F32)


def kernel(
    inputs, out_grad, w_up_hbm, w_down_hbm, ig_hbm, up_hbm, down_hbm,
    acts, w_up, w_down, own, give, take, low, r_in, p_in, q_in, total, z_out, z_in, held,
    partial, x_in, iz_out, iz_in, last, x_last, iz_out_last, iz_in_last, ig_out, up_out, down_out, acts_t,
    load_sem, store_sem, send_sem, recv_sem,
):
    row, col = lax.axis_index("row"), lax.axis_index("col")
    z_hi, y, c = row // 8, (row // 2) % 4, row % 2
    z_lo, x = col // 4, col % 4
    oc = 1 - c
    y_up, y_down, y_far = (y + 1) % 4, (y + 3) % 4, (y + 2) % 4
    in_row = lambda h, b, core: (h * 8 + b * 2 + core, col)
    in_col = lambda a, b: (row, a * 4 + b)
    up, down, other, pair = in_row(z_hi, y_up, c), in_row(z_hi, y_down, c), in_row(z_hi, y, oc), in_row(1 - z_hi, y, c)
    xs = [(x + d + 1) % 4 for d in range(3)]
    x_peers = [in_col(z_lo, b) for b in xs]
    flip = [z_lo, 3 - z_lo, (z_lo + 2) % 4, z_lo + 1 - 2 * (z_lo % 2)]
    plane_peers = [in_col(flip[k], x) for k in range(4)]

    weights = (w_up, w_down)
    sends = []

    def remote(name, src, dst, peer):
        i = SLOT[name]
        return pltpu.make_async_remote_copy(
            src_ref=src, dst_ref=dst, send_sem=send_sem.at[i], recv_sem=recv_sem.at[i], device_id=peer, device_id_type=MESH
        )

    def send(name, src, dst, peer):
        copy = remote(name, src, dst, peer)
        copy.start()
        sends.append(copy)

    def arrived(name, dst, peer):
        remote(name, dst, dst, peer).wait_recv()

    loads = [
        pltpu.make_async_copy(inputs, acts.at[0, pl.ds(x * BLOCK, BLOCK)], load_sem.at[0]),
        pltpu.make_async_copy(out_grad, acts.at[1, pl.ds(x * BLOCK, BLOCK)], load_sem.at[1]),
        pltpu.make_async_copy(w_up_hbm, w_up, load_sem.at[2]),
        pltpu.make_async_copy(w_down_hbm, w_down, load_sem.at[3]),
    ]
    for copy in loads:
        copy.start()

    barrier = pltpu.get_barrier_semaphore()
    everyone = [up, down, other, pair] + x_peers + plane_peers[1:]
    for peer in everyone:
        pl.semaphore_signal(barrier, inc=1, device_id=peer, device_id_type=MESH)
    pl.semaphore_wait(barrier, len(everyone))

    def mine(k, b):
        return acts.at[:, pl.ds(k * CHUNK + b * BLOCK, BLOCK)]

    def rows(k, b):
        return pl.ds(k * CHUNK + b * BLOCK, BLOCK)

    def block(b):
        return pl.ds(pl.multiple_of(b * BLOCK, BLOCK), BLOCK)

    def mine1(k, m, b):
        return acts.at[m, pl.ds(k * CHUNK + b * BLOCK, BLOCK)]

    def along_x(k, m):
        for d in (1, 0, 2):
            send(f"gx{k}{m}{d}", mine1(k, m, x), mine1(k, m, x), x_peers[d])

    for m in range(2):
        loads[m].wait()
        along_x(0, m)
    for k in (1, 2, 3):
        send(f"gz{k}", mine(0, x), mine(k, x), plane_peers[k])

    def P(k):
        arrived(f"gz{k}", mine(k, x), plane_peers[k])
        for m in range(2):
            along_x(k, m)

    def U(k, m):
        for d in range(3):
            arrived(f"gx{k}{m}{d}", mine1(k, m, xs[2 - d]), x_peers[d])
        if k == 0:
            loads[2 + m].wait()
        a = acts[m, k * CHUNK : (k + 1) * CHUNK, :]
        for half, into in ((oc, give), (c, own)):
            at = pl.ds(pl.multiple_of(half * HALF, 128), HALF)
            into[k, m] = jnp.dot(a, weights[m][:, at], preferred_element_type=F32)
            if into is give:
                send(f"c{k}{m}", give.at[k, m], take.at[k, m], other)

    def both(k, m, b):
        return own[k, m, block(b), :] + take[k, m, block(b), :]

    def C(k, m):
        arrived(f"c{k}{m}", take.at[k, m], other)
        far_peer, near_name, near, near_peer, near_in = ((up, "q", y_down, down, q_in), (down, "p", y_up, up, p_in))[m]
        low[k, m, block(y_far), :] = both(k, m, y_far).astype(BF16)
        send(f"r{k}{m}", low.at[k, m, block(y_far)], r_in.at[k, m], far_peer)
        low[k, m, block(near), :] = both(k, m, near).astype(BF16)
        send(f"{near_name}{k}{m}", low.at[k, m, block(near)], near_in.at[k, m], near_peer)

    def R(k, m):
        source, name, to, peer, into = ((down, "p", y_up, up, p_in), (up, "q", y_down, down, q_in))[m]
        arrived(f"r{k}{m}", r_in.at[k, m], source)
        low[k, m, block(to), :] = (both(k, m, to) + r_in[k, m].astype(F32)).astype(BF16)
        send(f"{name}{k}{m}", low.at[k, m, block(to)], into.at[k, m], peer)

    def Z(k, m):
        arrived(f"p{k}{m}", p_in.at[k, m], down)
        arrived(f"q{k}{m}", q_in.at[k, m], up)
        summed = both(k, m, y) + p_in[k, m].astype(F32) + q_in[k, m].astype(F32)
        total[k, m] = summed
        z_out[k, m] = summed.astype(BF16)
        send(f"z{k}{m}", z_out.at[k, m], z_in.at[k, m], pair)

    def A(k, m):
        arrived(f"z{k}{m}", z_in.at[k, m], pair)
        positive = jnp.maximum(total[k, 0] + z_in[k, 0].astype(F32), 0.0)
        if m == 0:
            held[0, c, rows(k, y), :] = (positive * positive).astype(BF16)
        else:
            hidden_grad = total[k, 1] + z_in[k, 1].astype(F32)
            held[1, c, rows(k, y), :] = (hidden_grad * 2.0 * positive).astype(BF16)
        here = held.at[m, c, rows(k, y)]
        send(f"au{k}{m}", here, here, up)
        send(f"ad{k}{m}", here, here, down)
        send(f"ac{k}{m}", here, here, other)

    def F(k, m):
        name, b, source, peer = (("au", y_down, down, up), ("ad", y_up, up, down))[m]
        there = held.at[m, c, rows(k, b)]
        arrived(f"{name}{k}{m}", there, source)
        send(f"f{k}{m}", there, there, peer)
        send(f"fc{k}{m}", there, there, other)

    def H(k, m):
        name, b, source = (("ad", y_up, up), ("au", y_down, down))[m]
        there = held.at[m, c, rows(k, b)]
        arrived(f"{name}{k}{m}", there, source)
        send(f"hc{k}{m}", there, there, other)

    def E(k, m):
        far = held.at[m, c, rows(k, y_far)]
        arrived(f"f{k}{m}", far, (down, up)[m])
        send(f"ec{k}{m}", far, far, other)

    def whole(k, m):
        arrived(f"ac{k}{m}", held.at[m, oc, rows(k, y)], other)
        arrived(f"fc{k}{m}", held.at[m, oc, rows(k, (y_down, y_up)[m])], other)
        arrived(f"hc{k}{m}", held.at[m, oc, rows(k, (y_up, y_down)[m])], other)
        arrived(f"ec{k}{m}", held.at[m, oc, rows(k, y_far)], other)

    def I(k):
        whole(k, 1)
        at = slice(k * CHUNK, (k + 1) * CHUNK)
        partial[k] = nt(held[1, 0, at, :], w_up[:, :HALF]) + nt(held[1, 1, at, :], w_up[:, HALF:])
        if k == 3:
            last[...] = partial[k].astype(BF16)
        for d in (1, 0, 2):
            if k == 3:
                send(f"ix{k}{d}", last.at[block(xs[d])], x_last.at[d], x_peers[d])
            else:
                send(f"ix{k}{d}", partial.at[k, block(xs[d])], x_in.at[k, d], x_peers[d])

    def J(k):
        landed = x_last if k == 3 else x_in.at[k]
        for d in range(3):
            arrived(f"ix{k}{d}", landed.at[d], x_peers[d])
        summed = partial[k, block(x), :]
        for d in range(3):
            summed = summed + landed[d].astype(F32)
        if k == 0:
            partial[k, block(x), :] = summed
        elif k == 3:
            iz_out_last[...] = summed.astype(BF16)
            send(f"iz{k}", iz_out_last, iz_in_last, plane_peers[k])
        else:
            iz_out[k - 1] = summed
            send(f"iz{k}", iz_out.at[k - 1], iz_in.at[k - 1], plane_peers[k])

    stores = []

    def store(src, dst):
        copy = pltpu.make_async_copy(src, dst, store_sem.at[len(stores)])
        copy.start()
        stores.append(copy)

    def T():
        for m in range(2):
            acts_t[m] = acts[m].T

    def G(m):
        out, dst = ((down_out, down_hbm), (up_out, up_hbm))[m]
        if m == 0:
            for k in range(4):
                whole(k, 0)
        for h in range(2):
            at = pl.ds(h * HALF, HALF)
            out[:, at] = jnp.dot(acts_t[1 - m], held[m, h], preferred_element_type=F32).astype(BF16)
            store(out.at[:, at], dst.at[:, at])

    stages = dict(P=P, U=U, C=C, R=R, Z=Z, A=A, F=F, H=H, E=E, I=I, J=J, T=T, G=G)
    for item in ORDER:
        stages[item[0]](*map(int, item[1:]))

    summed = partial[0, block(x), :]
    for k in (1, 2):
        arrived(f"iz{k}", iz_in.at[k - 1], plane_peers[k])
        summed = summed + iz_in[k - 1]
    arrived("iz3", iz_in_last, plane_peers[3])
    summed = summed + iz_in_last[...].astype(F32)
    ig_out[...] = summed.astype(BF16)
    store(ig_out, ig_hbm)
    for copy in sends:
        copy.wait_send()
    for copy in stores:
        copy.wait()


def shards(inputs, out_grad, w_up, w_down):
    anywhere = pl.BlockSpec(memory_space=pl.ANY)
    n = len(NAMES)
    input_grad, up_grad, down_grad_t = pl.pallas_call(
        kernel,
        out_shape=(
            jax.ShapeDtypeStruct((BLOCK, FEATS), BF16),
            jax.ShapeDtypeStruct((FEATS, 2 * HALF), BF16),
            jax.ShapeDtypeStruct((FEATS, 2 * HALF), BF16),
        ),
        in_specs=[anywhere] * 4,
        out_specs=(anywhere,) * 3,
        scratch_shapes=[
            pltpu.VMEM((2, PLANES * CHUNK, FEATS), BF16),
            pltpu.VMEM((FEATS, 2 * HALF), BF16),
            pltpu.VMEM((FEATS, 2 * HALF), BF16),
            pltpu.VMEM((PLANES, 2, CHUNK, HALF), F32),
            pltpu.VMEM((PLANES, 2, CHUNK, HALF), F32),
            pltpu.VMEM((PLANES, 2, CHUNK, HALF), F32),
            pltpu.VMEM((PLANES, 2, CHUNK, HALF), BF16),
            pltpu.VMEM((PLANES, 2, BLOCK, HALF), BF16),
            pltpu.VMEM((PLANES, 2, BLOCK, HALF), BF16),
            pltpu.VMEM((PLANES, 2, BLOCK, HALF), BF16),
            pltpu.VMEM((PLANES, 2, BLOCK, HALF), F32),
            pltpu.VMEM((PLANES, 2, BLOCK, HALF), BF16),
            pltpu.VMEM((PLANES, 2, BLOCK, HALF), BF16),
            pltpu.VMEM((2, 2, PLANES * CHUNK, HALF), BF16),
            pltpu.VMEM((PLANES, CHUNK, FEATS), F32),
            pltpu.VMEM((3, 3, BLOCK, FEATS), F32),
            pltpu.VMEM((2, BLOCK, FEATS), F32),
            pltpu.VMEM((2, BLOCK, FEATS), F32),
            pltpu.VMEM((CHUNK, FEATS), BF16),
            pltpu.VMEM((3, BLOCK, FEATS), BF16),
            pltpu.VMEM((BLOCK, FEATS), BF16),
            pltpu.VMEM((BLOCK, FEATS), BF16),
            pltpu.VMEM((BLOCK, FEATS), BF16),
            pltpu.VMEM((FEATS, 2 * HALF), BF16),
            pltpu.VMEM((FEATS, 2 * HALF), BF16),
            pltpu.VMEM((2, FEATS, PLANES * CHUNK), BF16),
            pltpu.SemaphoreType.DMA((4,)),
            pltpu.SemaphoreType.DMA((5,)),
            pltpu.SemaphoreType.DMA((n,)),
            pltpu.SemaphoreType.DMA((n,)),
        ],
        compiler_params=pltpu.CompilerParams(collective_id=0, has_side_effects=True, vmem_limit_bytes=60 * 2**20),
        cost_estimate=pl.CostEstimate(flops=6_800_000_000, bytes_accessed=11_000_000, transcendentals=0),
        name="ffn_backward",
    )(inputs, out_grad, w_up, w_down.T)
    return input_grad, up_grad, down_grad_t.T


def solution(mesh):
    in_specs = (P("col", "row"), P("col", "row"), P("row", "col"), P("col", "row"))
    out_specs = (P("col", "row"), P("row", "col"), P("col", "row"))
    return jax.shard_map(shards, mesh=mesh, in_specs=in_specs, out_specs=out_specs, check_vma=False)
```

time: 495 us -> 88.8 us (0.18)
  the two profiles are of different devices: /device:TPU:16 before, /device:TPU:1 now
where the time goes in v1:
time: 88.8 us; the launch traced here: 88.7 us
  Pallas kernels  81.5 us (92%)
  local copies, waits for them, and re-layouts  6.48 us (7%)
    pallas_call x1, Pallas kernels, shards(): pl.pallas_call(kernel, out_shape=(jax.ShapeDtypeStruct((BLOCK, FEATS), BF...  81.5 us
    unnamed x5, local copies, waits for them, and re-layouts  6.48 us

profile of v1, /device:TPU:1, one launch (start us, length us, event | category | flops | bytes accessed | tf_op | source)
XLA Modules:
  0.0 88.7 jit_solution(15773206779315653709)
XLA Ops:
  0.6 81.5 %ffn_backward.1 = (bf16[32,576]{1,0:T(8,128)(2,1)}, bf16[576,2304]{1,0:T(8,128)(2,1)}, bf16[576,2304]{1,0:T(8,128)(2,1)}) custom-call(bf16[32,576]{1,0:T(8,128)(2,1)} %inputs.1, bf16[32,576]{1,0:T(8,128)(2,1)} %out_grad.1, bf16[576,2304]{1,0:T(8,128)(2,1)} %w_up_hbm.1, bf16[576,2304]{1,0:T(8,128)(2,1)} %bitcast.3), custom_call_target="tpu_custom_call" | custom-call | flops 6800000000 | bytes 11000000 | tf_op jit(solution)/shard_map/ffn_backward/pallas_call | solution.py:279
  82.2 1.4 %copy.10 = bf16[32,576]{1,0:T(8,128)(2,1)} copy(bf16[32,576]{1,0:T(8,128)(2,1)} %get-tuple-element.12) | data formatting | bytes 73728
  83.6 0.0 copy-start
  83.6 3.6 %copy.11 = bf16[576,2304]{1,0:T(8,128)(2,1)} copy(bf16[576,2304]{1,0:T(8,128)(2,1)} %get-tuple-element.13) | data formatting | bytes 5308416
  87.2 0.0 copy-done
  87.2 1.5 %copy.12 = bf16[2304,576]{0,1:T(8,128)(2,1)} copy(bf16[2304,576]{0,1:T(8,128)(2,1)S(1)} %bitcast.2) | data formatting | bytes 5308416
Async XLA Ops:
  83.6 3.6 %copy-start = (bf16[576,2304]{1,0:T(8,128)(2,1)S(1)}, bf16[576,2304]{1,0:T(8,128)(2,1)}, u32[]{:S(2)}) copy-start(bf16[576,2304]{1,0:T(8,128)(2,1)} %get-tuple-element.8) | copy-start | bytes 7962628

commit v2 on v1

--- a/solution.py
+++ b/solution.py
@@ -17,33 +17,34 @@
 HALF = 1152
 
 ORDER = (
-    "U00 U01 C00 P1".split()
-    + "P2 C01 P3 R00".split()
-    + "U10 R01 U11 C10".split()
-    + "U20 Z00 C11 U21".split()
-    + "Z01 C20 R10 U30".split()
-    + "C21 U31 R11 C30".split()
-    + "R20 C31 A00 Z10".split()
-    + "R21 Z11 T A01".split()
-    + "R30 Z20 R31 A10".split()
-    + "H00 F00 Z21 H01".split()
-    + "A11 F01 Z30 Z31".split()
-    + "A20 F10 H10 E00".split()
-    + "F11 A21 H11 E01".split()
-    + "I0 F20 H20 A30".split()
-    + "E10 E11 I1 A31".split()
-    + "H21 F21 E20 H30".split()
-    + "J0 F30 F31 H31".split()
-    + "J1 E21 E30 I2".split()
-    + "E31 I3 G0 J2".split()
-    + "J3 G1".split()
+    "P1 U00 P2 U01".split()
+    + "C00 U10 C01 U11".split()
+    + "R00 P3 C10 U20".split()
+    + "R01 C11 C20 U21".split()
+    + "Z00 R10 Z01 C21".split()
+    + "U30 U31 R11 R20".split()
+    + "Z10 C31 R21 C30".split()
+    + "Z11 R31 Z20 A00".split()
+    + "R30 A01 Z21 Z31".split()
+    + "A11 A10 F01 Z30".split()
+    + "F11 H01 A21 A20".split()
+    + "E01 F10 E11 A31".split()
+    + "H11 I0 F21 H20".split()
+    + "I1 H21 T H10".split()
+    + "F31 H31 E21 A30".split()
+    + "F20 I2 F00 E31".split()
+    + "E10 F30 I3 H30".split()
+    + "H00 J1 G1 J2".split()
+    + "E20 E00 J0 E30".split()
+    + "J3 G0".split()
 )
+
 
 NAMES = (
     [f"gz{k}" for k in (1, 2, 3)]
     + [f"gx{k}{m}{d}" for k in range(4) for m in range(2) for d in range(3)]
-    + [f"{s}{k}{m}" for s in "c r p q z au ad".split() for k in range(4) for m in range(2)]
-    + [f"{s}{k}{m}" for s in "ac f fc hc ec".split() for k in range(4) for m in range(2)]
+    + [f"{s}{k}{m}" for s in ("c", "r", "p", "q", "z", "au", "ad") for k in range(4) for m in range(2)]
+    + [f"{s}{k}{m}" for s in ("ac", "f", "fc", "hc", "ec") for k in range(4) for m in range(2)]
     + [f"ix{k}{d}" for k in range(4) for d in range(3)]
     + [f"iz{k}" for k in (1, 2, 3)]
 )
@@ -74,7 +75,7 @@
     plane_peers = [in_col(flip[k], x) for k in range(4)]
 
     weights = (w_up, w_down)
-    sends = []
+    sends, seen = [], set()
 
     def remote(name, src, dst, peer):
         i = SLOT[name]
@@ -88,6 +89,9 @@
         sends.append(copy)
 
     def arrived(name, dst, peer):
+        if name in seen:
+            return
+        seen.add(name)
         remote(name, dst, dst, peer).wait_recv()
 
     loads = [
@@ -170,7 +174,8 @@
         send(f"z{k}{m}", z_out.at[k, m], z_in.at[k, m], pair)
 
     def A(k, m):
-        arrived(f"z{k}{m}", z_in.at[k, m], pair)
+        for p in range(m + 1):
+            arrived(f"z{k}{p}", z_in.at[k, p], pair)
         positive = jnp.maximum(total[k, 0] + z_in[k, 0].astype(F32), 0.0)
         if m == 0:
             held[0, c, rows(k, y), :] = (positive * positive).astype(BF16)
@@ -273,6 +278,18 @@
         copy.wait()
 
 
+def hand_over(ig, up, down, ig_to, up_to, down_to, sem):
+    copies = [pltpu.make_async_copy(ig, ig_to, sem.at[8])]
+    for i in range(4):
+        at = pl.ds(i * 144, 144)
+        copies.append(pltpu.make_async_copy(up.at[at], up_to.at[at], sem.at[i]))
+        copies.append(pltpu.make_async_copy(down.at[at], down_to.at[at], sem.at[4 + i]))
+    for copy in copies:
+        copy.start()
+    for copy in copies:
+        copy.wait()
+
+
 def shards(inputs, out_grad, w_up, w_down):
     anywhere = pl.BlockSpec(memory_space=pl.ANY)
     n = len(NAMES)
@@ -283,7 +300,7 @@
             jax.ShapeDtypeStruct((FEATS, 2 * HALF), BF16),
             jax.ShapeDtypeStruct((FEATS, 2 * HALF), BF16),
         ),
-        in_specs=[anywhere] * 4,
+        in_specs=[pl.BlockSpec(memory_space=pltpu.HBM)] * 4,
         out_specs=(anywhere,) * 3,
         scratch_shapes=[
             pltpu.VMEM((2, PLANES * CHUNK, FEATS), BF16),
@@ -317,10 +334,20 @@
             pltpu.SemaphoreType.DMA((n,)),
             pltpu.SemaphoreType.DMA((n,)),
         ],
-        compiler_params=pltpu.CompilerParams(collective_id=0, has_side_effects=True, vmem_limit_bytes=60 * 2**20),
+        compiler_params=pltpu.CompilerParams(collective_id=0, has_side_effects=True, vmem_limit_bytes=46 * 2**20),
         cost_estimate=pl.CostEstimate(flops=6_800_000_000, bytes_accessed=11_000_000, transcendentals=0),
         name="ffn_backward",
-    )(inputs, out_grad, w_up, w_down.T)
+    )(*(pltpu.with_memory_space_constraint(a, pltpu.HBM) for a in (inputs, out_grad, w_up, w_down.T)))
+    input_grad, up_grad, down_grad_t = pl.pallas_call(
+        hand_over,
+        out_shape=tuple(jax.ShapeDtypeStruct(a.shape, a.dtype) for a in (input_grad, up_grad, down_grad_t)),
+        in_specs=[anywhere] * 3,
+        out_specs=(anywhere,) * 3,
+        scratch_shapes=[pltpu.SemaphoreType.DMA((9,))],
+        compiler_params=pltpu.CompilerParams(vmem_limit_bytes=2 * 2**20),
+        cost_estimate=pl.CostEstimate(flops=0, bytes_accessed=10_700_000, transcendentals=0),
+        name="hand_over",
+    )(input_grad, up_grad, down_grad_t)
     return input_grad, up_grad, down_grad_t.T
 
 

time: 88.8 us -> 80.5 us (0.907)
  local copies, waits for them, and re-layouts: 6.48 us -> 0 us
  Pallas kernels: 81.5 us -> 79.6 us
    unnamed x5 -> x0, local copies, waits for them, and re-layouts: 6.48 us -> none
    pallas_call x1, Pallas kernels: 81.5 us -> 77.1 us  [shards(): pl.pallas_call(kernel, out_shape=(jax.ShapeDtypeStruct((BLOCK, FEATS), BF...]
    pallas_call x0 -> x1, Pallas kernels: none -> 2.46 us  [shards(): pl.pallas_call(hand_over, out_shape=tuple((jax.ShapeDtypeStruct(a.shape,...]
where the time goes in v2:
time: 80.5 us; the launch traced here: 80.4 us
  Pallas kernels  79.6 us (99%)
    pallas_call x1, Pallas kernels, shards(): pl.pallas_call(kernel, out_shape=(jax.ShapeDtypeStruct((BLOCK, FEATS), BF...  77.1 us
    pallas_call x1, Pallas kernels, shards(): pl.pallas_call(hand_over, out_shape=tuple((jax.ShapeDtypeStruct(a.shape,...  2.46 us

profile of v2, /device:TPU:1, one launch (start us, length us, event | category | flops | bytes accessed | tf_op | source)
XLA Modules:
  0.0 80.4 jit_solution(16894001195138209669)
XLA Ops:
  0.6 77.1 %ffn_backward.1 = (bf16[32,576]{1,0:T(8,128)(2,1)S(1)}, bf16[576,2304]{1,0:T(8,128)(2,1)S(1)}, bf16[576,2304]{1,0:T(8,128)(2,1)S(1)}) custom-call(bf16[32,576]{1,0:T(8,128)(2,1)} %inputs.1, bf16[32,576]{1,0:T(8,128)(2,1)} %out_grad.1, bf16[576,2304]{1,0:T(8,128)(2,1)} %w_up_hbm.1, bf16[576,2304]{1,0:T(8,128)(2,1)} %bitcast.2), custom_call_target="tpu_custom_call" | custom-call | flops 6800000000 | bytes 11000000 | tf_op jit(solution)/shard_map/ffn_backward/pallas_call | solution.py:296
  77.8 2.5 %hand_over.1 = (bf16[32,576]{1,0:T(8,128)(2,1)}, bf16[576,2304]{1,0:T(8,128)(2,1)}, bf16[576,2304]{1,0:T(8,128)(2,1)}) custom-call(bf16[32,576]{1,0:T(8,128)(2,1)S(1)} %get-tuple-element.9.ig, bf16[576,2304]{1,0:T(8,128)(2,1)S(1)} %get-tuple-element.10.up, bf16[576,2304]{1,0:T(8,128)(2,1)S(1)} %get-tuple-element.11.down), custom_call_target="tpu_custom_call" | custom-call | bytes 10700000 | tf_op jit(solution)/shard_map/hand_over/pallas_call | solution.py:341

commit v3 on v2

--- a/solution.py
+++ b/solution.py
@@ -56,9 +56,9 @@
 
 
 def kernel(
-    inputs, out_grad, w_up_hbm, w_down_hbm, ig_hbm, up_hbm, down_hbm,
+    inputs, out_grad, w_up_hbm, w_down_hbm, ig_hbm, up_out, down_out,
     acts, w_up, w_down, own, give, take, low, r_in, p_in, q_in, total, z_out, z_in, held,
-    partial, x_in, iz_out, iz_in, last, x_last, iz_out_last, iz_in_last, ig_out, up_out, down_out, acts_t,
+    partial, x_in, iz_out, iz_in, last, x_last, iz_out_last, iz_in_last, ig_out, acts_t,
     load_sem, store_sem, send_sem, recv_sem,
 ):
     row, col = lax.axis_index("row"), lax.axis_index("col")
@@ -251,19 +251,20 @@
             acts_t[m] = acts[m].T
 
     def G(m):
-        out, dst = ((down_out, down_hbm), (up_out, up_hbm))[m]
+        out = (down_out, up_out)[m]
         if m == 0:
             for k in range(4):
                 whole(k, 0)
         for h in range(2):
             at = pl.ds(h * HALF, HALF)
             out[:, at] = jnp.dot(acts_t[1 - m], held[m, h], preferred_element_type=F32).astype(BF16)
-            store(out.at[:, at], dst.at[:, at])
 
     stages = dict(P=P, U=U, C=C, R=R, Z=Z, A=A, F=F, H=H, E=E, I=I, J=J, T=T, G=G)
     for item in ORDER:
         stages[item[0]](*map(int, item[1:]))
 
+    for copy in sends[:-4]:
+        copy.wait_send()
     summed = partial[0, block(x), :]
     for k in (1, 2):
         arrived(f"iz{k}", iz_in.at[k - 1], plane_peers[k])
@@ -272,18 +273,15 @@
     summed = summed + iz_in_last[...].astype(F32)
     ig_out[...] = summed.astype(BF16)
     store(ig_out, ig_hbm)
-    for copy in sends:
+    for copy in sends[-4:]:
         copy.wait_send()
     for copy in stores:
         copy.wait()
 
 
 def hand_over(ig, up, down, ig_to, up_to, down_to, sem):
-    copies = [pltpu.make_async_copy(ig, ig_to, sem.at[8])]
-    for i in range(4):
-        at = pl.ds(i * 144, 144)
-        copies.append(pltpu.make_async_copy(up.at[at], up_to.at[at], sem.at[i]))
-        copies.append(pltpu.make_async_copy(down.at[at], down_to.at[at], sem.at[4 + i]))
+    pairs = ((up, up_to), (down, down_to), (ig, ig_to))
+    copies = [pltpu.make_async_copy(a, b, sem.at[i]) for i, (a, b) in enumerate(pairs)]
     for copy in copies:
         copy.start()
     for copy in copies:
@@ -301,7 +299,7 @@
             jax.ShapeDtypeStruct((FEATS, 2 * HALF), BF16),
         ),
         in_specs=[pl.BlockSpec(memory_space=pltpu.HBM)] * 4,
-        out_specs=(anywhere,) * 3,
+        out_specs=(anywhere,) + (pl.BlockSpec(memory_space=pltpu.VMEM),) * 2,
         scratch_shapes=[
             pltpu.VMEM((2, PLANES * CHUNK, FEATS), BF16),
             pltpu.VMEM((FEATS, 2 * HALF), BF16),
@@ -326,11 +324,9 @@
             pltpu.VMEM((BLOCK, FEATS), BF16),
             pltpu.VMEM((BLOCK, FEATS), BF16),
             pltpu.VMEM((BLOCK, FEATS), BF16),
-            pltpu.VMEM((FEATS, 2 * HALF), BF16),
-            pltpu.VMEM((FEATS, 2 * HALF), BF16),
             pltpu.VMEM((2, FEATS, PLANES * CHUNK), BF16),
             pltpu.SemaphoreType.DMA((4,)),
-            pltpu.SemaphoreType.DMA((5,)),
+            pltpu.SemaphoreType.DMA((1,)),
             pltpu.SemaphoreType.DMA((n,)),
             pltpu.SemaphoreType.DMA((n,)),
         ],
@@ -343,7 +339,7 @@
         out_shape=tuple(jax.ShapeDtypeStruct(a.shape, a.dtype) for a in (input_grad, up_grad, down_grad_t)),
         in_specs=[anywhere] * 3,
         out_specs=(anywhere,) * 3,
-        scratch_shapes=[pltpu.SemaphoreType.DMA((9,))],
+        scratch_shapes=[pltpu.SemaphoreType.DMA((3,))],
         compiler_params=pltpu.CompilerParams(vmem_limit_bytes=2 * 2**20),
         cost_estimate=pl.CostEstimate(flops=0, bytes_accessed=10_700_000, transcendentals=0),
         name="hand_over",

time: 80.5 us -> 79.9 us (level)
  no operation moved by 1% of the time
where the time goes in v3:
time: 79.9 us; the launch traced here: 79.4 us
  Pallas kernels  78.8 us (99%)
    pallas_call x1, Pallas kernels, shards(): pl.pallas_call(kernel, out_shape=(jax.ShapeDtypeStruct((BLOCK, FEATS), BF...  76.4 us
    pallas_call x1, Pallas kernels, shards(): pl.pallas_call(hand_over, out_shape=tuple((jax.ShapeDtypeStruct(a.shape,...  2.41 us

profile of v3, /device:TPU:1, one launch (start us, length us, event | category | flops | bytes accessed | tf_op | source)
XLA Modules:
  0.0 79.4 jit_solution(5455825870055186477)
XLA Ops:
  0.6 76.4 %ffn_backward.1 = (bf16[32,576]{1,0:T(8,128)(2,1)S(1)}, bf16[576,2304]{1,0:T(8,128)(2,1)S(1)}, bf16[576,2304]{1,0:T(8,128)(2,1)S(1)}) custom-call(bf16[32,576]{1,0:T(8,128)(2,1)} %inputs.1, bf16[32,576]{1,0:T(8,128)(2,1)} %out_grad.1, bf16[576,2304]{1,0:T(8,128)(2,1)} %w_up_hbm.1, bf16[576,2304]{1,0:T(8,128)(2,1)} %bitcast.2), custom_call_target="tpu_custom_call" | custom-call | flops 6800000000 | bytes 11000000 | tf_op jit(solution)/shard_map/ffn_backward/pallas_call | solution.py:294
  77.0 2.4 %hand_over.1 = (bf16[32,576]{1,0:T(8,128)(2,1)}, bf16[576,2304]{1,0:T(8,128)(2,1)}, bf16[576,2304]{1,0:T(8,128)(2,1)}) custom-call(bf16[32,576]{1,0:T(8,128)(2,1)S(1)} %get-tuple-element.9.ig, bf16[576,2304]{1,0:T(8,128)(2,1)S(1)} %get-tuple-element.10.up, bf16[576,2304]{1,0:T(8,128)(2,1)S(1)} %get-tuple-element.11.down), custom_call_target="tpu_custom_call" | custom-call | bytes 10700000 | tf_op jit(solution)/shard_map/hand_over/pallas_call | solution.py:337
